TPU v7x, 32 devices: a whole 2x2x4 slice. The times are simulated.
32 devices in a mesh: loop: 16 (over z, x, core), tok: 2 (over y).
Axes of the slice: x: 2, y: 2, z: 4, core: 2. Of those that a mesh axis runs over, the one named last changes fastest.
Arguments:
- features: bfloat16 [2048, 4096], P('loop', 'tok'), may hold values from -6 to 6
- expert_rows: int32 [2, 768], replicated, may hold values from 0 to 2047, as said below
- route_weight: float32 [2, 768], replicated, may hold values from 0.1 to 1
- gate_proj: bfloat16 [2, 4096, 14336], P(None, 'tok', 'loop'), may hold values from -0.09375 to 0.09375
- up_proj: bfloat16 [2, 4096, 14336], P(None, 'tok', 'loop'), may hold values from -0.09375 to 0.09375
- down_proj: bfloat16 [2, 14336, 4096], P(None, 'loop', 'tok'), may hold values from -0.046875 to 0.046875
- out_grad: bfloat16 [2048, 4096], P('loop', 'tok'), may hold values from -6 to 6
Outputs:
- mixed: bfloat16 [2048, 4096], P('loop', 'tok')
- feature_grad: bfloat16 [2048, 4096], P('loop', 'tok')
- gate_grad: bfloat16 [2, 4096, 14336], P(None, 'tok', 'loop')
- up_grad: bfloat16 [2, 4096, 14336], P(None, 'tok', 'loop')
- down_grad: bfloat16 [2, 14336, 4096], P(None, 'loop', 'tok')
Inputs may be any that keep to these rules, and one draw needn't show every extreme that they name: `expert_rows`: each expert's list holds 768 distinct tokens in ascending order, and tokens 0 and 2047 are in every list. Of the 128 tokens t with the same t // 128, at most 96 are in one list, and in every list exactly 96 come from one such index.
All inputs are finite; a program needn't handle non-finite values.
Results may differ from a plain program's by a relative error of at most 0.0049.
Values may be sent and summed in bfloat16 or wider, within the bound.
No kernel may reach another device: no remote copies, remote signals or barrier semaphores. Data moves between devices by JAX's collectives and lax.ppermute only.
A program may use at most 192 MiB of HBM per device.

v0:
```python
import jax
import jax.numpy as jnp
from jax import lax
from jax.sharding import PartitionSpec as P


def local_grads(back, weights, gate, upval):
    weighted = weights[:, :, None] * back
    sigma = jax.nn.sigmoid(gate)
    gate_bar = (weighted * upval * sigma * (1.0 + gate * (1.0 - sigma))).astype(jnp.bfloat16)
    up_bar = (weighted * gate * sigma).astype(jnp.bfloat16)
    return (gate_bar, up_bar)


def local(features, expert_rows, route_weight, gate_proj, up_proj, down_proj, out_grad):
    loop_size = lax.axis_size("loop")
    tok_size = lax.axis_size("tok")
    tok_index = lax.axis_index("tok")
    local_tokens = features.shape[0]
    width = features.shape[1]
    rows_each = expert_rows.shape[1]
    total_tokens = local_tokens * loop_size
    flat_rows = expert_rows.reshape(-1)
    everyone = lax.all_gather(features, "loop", axis=0, tiled=True)
    token_rows = everyone[expert_rows]
    gate_part = jnp.einsum(
        "erd,edf->erf", token_rows, gate_proj, preferred_element_type=jnp.float32
    )
    up_part = jnp.einsum("erd,edf->erf", token_rows, up_proj, preferred_element_type=jnp.float32)
    share = rows_each // tok_size
    gate_share, up_share = (
        lax.psum_scatter(gate_part, "tok", scatter_dimension=1, tiled=True),
        lax.psum_scatter(up_part, "tok", scatter_dimension=1, tiled=True),
    )
    weight_share = lax.dynamic_slice_in_dim(route_weight, tok_index * share, share, 1)
    scaled_share = (weight_share[:, :, None] * jax.nn.silu(gate_share) * up_share).astype(
        jnp.bfloat16
    )
    scaled = lax.all_gather(scaled_share, "tok", axis=1, tiled=True)
    expert_out = jnp.einsum("erf,efd->erd", scaled, down_proj, preferred_element_type=jnp.float32)
    out_buffer = (
        jnp.zeros((total_tokens, width), jnp.float32)
        .at[flat_rows]
        .add(expert_out.reshape(-1, width))
    )
    mixed = lax.psum_scatter(out_buffer, "loop", scatter_dimension=0, tiled=True).astype(
        jnp.bfloat16
    )
    grad_everyone = lax.all_gather(out_grad, "loop", axis=0, tiled=True)
    grad_rows = grad_everyone[expert_rows]
    back_part = jnp.einsum("erd,efd->erf", grad_rows, down_proj, preferred_element_type=jnp.float32)
    back_share = lax.psum_scatter(back_part, "tok", scatter_dimension=1, tiled=True)
    gate_bar_share, up_bar_share = local_grads(back_share, weight_share, gate_share, up_share)
    gate_bar, up_bar = (
        lax.all_gather(gate_bar_share, "tok", axis=1, tiled=True),
        lax.all_gather(up_bar_share, "tok", axis=1, tiled=True),
    )
    input_part = jnp.einsum("erf,edf->erd", gate_bar, gate_proj, preferred_element_type=jnp.float32)
    input_part = input_part + jnp.einsum(
        "erf,edf->erd", up_bar, up_proj, preferred_element_type=jnp.float32
    )
    grad_buffer = (
        jnp.zeros((total_tokens, width), jnp.float32)
        .at[flat_rows]
        .add(input_part.reshape(-1, width))
    )
    feature_grad = lax.psum_scatter(grad_buffer, "loop", scatter_dimension=0, tiled=True).astype(
        jnp.bfloat16
    )
    gate_grad = jnp.einsum(
        "erd,erf->edf", token_rows, gate_bar, preferred_element_type=jnp.float32
    ).astype(jnp.bfloat16)
    up_grad = jnp.einsum(
        "erd,erf->edf", token_rows, up_bar, preferred_element_type=jnp.float32
    ).astype(jnp.bfloat16)
    down_grad = jnp.einsum(
        "erf,erd->efd", scaled, grad_rows, preferred_element_type=jnp.float32
    ).astype(jnp.bfloat16)
    return (mixed, feature_grad, gate_grad, up_grad, down_grad)


def solution(mesh):
    placed = (
        P("loop", "tok"),
        P(),
        P(),
        P(None, "tok", "loop"),
        P(None, "tok", "loop"),
        P(None, "loop", "tok"),
        P("loop", "tok"),
    )
    return jax.shard_map(
        local,
        mesh=mesh,
        in_specs=placed,
        out_specs=(
            P("loop", "tok"),
            P("loop", "tok"),
            P(None, "tok", "loop"),
            P(None, "tok", "loop"),
            P(None, "loop", "tok"),
        ),
        check_vma=False,
    )
```

profile of v0, /device:TPU:0, one launch (start us, length us, event | category | flops | bytes accessed | tf_op | source)
XLA Modules:
  0.0 881.3 jit_solution(9479926237028881631)
XLA Ops:
  7.2 0.7 all-gather.6.cloned.1.call-update
  8.0 0.7 all-gather.10.cloned.1.call-update
  8.7 0.7 compare_select_fusion.1
  9.4 78.4 %all-gather.6.cloned.1.call-done = bf16[2048,2048]{1,0:T(8,128)(2,1)} async-done(((bf16[128,2048]{1,0:T(8,128)(2,1)}), bf16[2048,2048]{1,0:T(8,128)(2,1)}) %all-gather.6.cloned.1.call-update) | async-done | bytes 8388624 | tf_op jit(solution)/shard_map/all_gather | solution.py:24
  87.8 17.2 %gather_fusion = bf16[1536,2048]{1,0:T(8,128)(2,1)} fusion(bf16[2048,2048]{1,0:T(8,128)(2,1)} %all-gather.6.cloned.1.call-done, s32[2048]{0:T(1024)S(1)} %pad_clamp_fusion), kind=kCustom, calls=%fused_computation | custom fusion | bytes 12589056 | tf_op jit(solution)/shard_map/gather | solution.py:25
  105.0 12.5 %fusion.5 = f32[2,768,896]{2,1,0:T(8,128)} fusion(bf16[2,768,2048]{2,1,0:T(8,128)(2,1)} %bitcast.26, bf16[2,2048,896]{2,1,0:T(8,128)(2,1)} %param.10), kind=kOutput, calls=%fused_computation.21 | convolution fusion | flops 5637144576 | bytes 19136512 | tf_op jit(solution)/shard_map/erd,edf->erf/dot_general | solution.py:26
  117.4 0.5 reduce-scatter.12.cloned.1.call-start
  117.9 45.2 %all-gather.10.cloned.1.call-done = bf16[2048,2048]{1,0:T(8,128)(2,1)} async-done(((bf16[128,2048]{1,0:T(8,128)(2,1)}), bf16[2048,2048]{1,0:T(8,128)(2,1)}) %all-gather.10.cloned.1.call-update) | async-done | bytes 8388624 | tf_op jit(solution)/shard_map/all_gather | solution.py:49
  163.1 17.2 %gather_fusion.1 = bf16[1536,2048]{1,0:T(8,128)(2,1)} fusion(bf16[2048,2048]{1,0:T(8,128)(2,1)} %all-gather.10.cloned.1.call-done, s32[2048]{0:T(1024)S(1)} %pad_clamp_fusion), kind=kCustom, calls=%fused_computation.1 | custom fusion | bytes 12589056 | tf_op jit(solution)/shard_map/gather | solution.py:50
  180.3 12.8 %fusion.8 = f32[2,768,896]{2,1,0:T(8,128)} fusion(bf16[2,768,2048]{2,1,0:T(8,128)(2,1)} %bitcast.32, bf16[2,896,2048]{2,1,0:T(8,128)(2,1)} %param.12), kind=kOutput, calls=%fused_computation.24 | convolution fusion | flops 5637144576 | bytes 19136512 | tf_op jit(solution)/shard_map/erd,efd->erf/dot_general | solution.py:51
  193.2 12.8 %fusion.6 = f32[2,768,896]{2,1,0:T(8,128)} fusion(bf16[2,768,2048]{2,1,0:T(8,128)(2,1)} %bitcast.27, bf16[2,2048,896]{2,1,0:T(8,128)(2,1)} %param.11), kind=kOutput, calls=%fused_computation.22 | convolution fusion | flops 5637144576 | bytes 19136512 | tf_op jit(solution)/shard_map/erd,edf->erf/dot_general | solution.py:29
  206.1 26.7 %reduce-scatter.6.cloned.1.call-done = f32[2,384,896]{2,1,0:T(8,128)} async-done(((f32[2,768,896]{2,1,0:T(8,128)}), f32[2,384,896]{2,1,0:T(8,128)}) %reduce-scatter.6.cloned.1.call-update) | async-done | bytes 2752528 | tf_op jit(solution)/shard_map/reduce_scatter | solution.py:32
  232.8 71.4 %reduce-scatter.12.cloned.1.call-done = f32[2,384,896]{2,1,0:T(8,128)} async-done(((f32[2,768,896]{2,1,0:T(8,128)}), f32[2,384,896]{2,1,0:T(8,128)}) %reduce-scatter.12.cloned.1.call-update) | async-done | bytes 2752528 | tf_op jit(solution)/shard_map/reduce_scatter | solution.py:52
  304.2 70.7 %reduce-scatter.8.cloned.1.call-done = f32[2,384,896]{2,1,0:T(8,128)} async-done(((f32[2,768,896]{2,1,0:T(8,128)}), f32[2,384,896]{2,1,0:T(8,128)}) %reduce-scatter.8.cloned.1.call-update) | async-done | bytes 2752528 | tf_op jit(solution)/shard_map/reduce_scatter | solution.py:33
  374.9 5.5 multiply_convert_fusion
  380.5 0.7 all-gather.12.cloned.1.call-update
  381.3 0.7 all-gather.14.cloned.1.call-update
  382.3 38.9 %all-gather.8.cloned.1.call-done = bf16[2,768,896]{2,1,0:T(8,128)(2,1)} async-done(((bf16[2,384,896]{2,1,0:T(8,128)(2,1)}), bf16[2,768,896]{2,1,0:T(8,128)(2,1)}) %all-gather.8.cloned.1.call-update) | async-done | bytes 2752528 | tf_op jit(solution)/shard_map/all_gather | solution.py:39
  421.2 12.4 %fusion.7 = f32[2,768,2048]{2,1,0:T(8,128)} fusion(bf16[2,768,896]{2,1,0:T(8,128)(2,1)} %all-gather.8.cloned.1.call-done, bf16[2,896,2048]{2,1,0:T(8,128)(2,1)} %param.12), kind=kOutput, calls=%fused_computation.23 | convolution fusion | flops 5637144576 | bytes 22675456 | tf_op jit(solution)/shard_map/erf,efd->erd/dot_general | solution.py:40
  433.5 27.7 %scatter_custom_fusion = f32[2048,2048]{1,0:T(8,128)} fusion(s32[1536]{0:T(1024)S(1)} %fusion.4, f32[1536,2048]{1,0:T(8,128)} %bitcast.39, f32[]{:T(128)} %constant.7.clone.1), kind=kCustom, calls=%fused_computation.6 | custom fusion | flops 3145728 | bytes 16777728 | tf_op jit(solution)/shard_map/scatter-add | solution.py:44
  461.5 2.4 all-gather.12.cloned.1.call-done
  463.9 12.4 %fusion.9 = f32[2,768,2048]{2,1,0:T(8,128)} fusion(bf16[2,768,896]{2,1,0:T(8,128)(2,1)} %all-gather.12.cloned.1.call-done, bf16[2,2048,896]{2,1,0:T(8,128)(2,1)} %param.10), kind=kOutput, calls=%fused_computation.25 | convolution fusion | flops 5637144576 | bytes 22675456 | tf_op jit(solution)/shard_map/erf,edf->erd/dot_general | solution.py:58
  476.3 30.3 %all-gather.14.cloned.1.call-done = bf16[2,768,896]{2,1,0:T(8,128)(2,1)} async-done(((bf16[2,384,896]{2,1,0:T(8,128)(2,1)}), bf16[2,768,896]{2,1,0:T(8,128)(2,1)}) %all-gather.14.cloned.1.call-update) | async-done | bytes 2752528 | tf_op jit(solution)/shard_map/all_gather | solution.py:56
  506.6 15.1 %convolution_add_fusion = f32[2,768,2048]{2,1,0:T(8,128)} fusion(f32[2,768,2048]{2,1,0:T(8,128)} %fusion.9, bf16[2,768,896]{2,1,0:T(8,128)(2,1)} %all-gather.14.cloned.1.call-done, bf16[2,2048,896]{2,1,0:T(8,128)(2,1)} %param.11), kind=kOutput, calls=%fused_computation.11 | convolution fusion | flops 5640290304 | bytes 35258368 | tf_op jit(solution)/shard_map/erf,edf->erd/dot_general | solution.py:59
  521.7 29.2 %scatter_custom_fusion.1 = f32[2048,2048]{1,0:T(8,128)} fusion(s32[1536]{0:T(1024)S(1)} %fusion.4, f32[1536,2048]{1,0:T(8,128)} %bitcast.38, f32[]{:T(128)} %constant.7.clone.1), kind=kCustom, calls=%fused_computation.4 | custom fusion | flops 3145728 | bytes 16777728 | tf_op jit(solution)/shard_map/scatter-add | solution.py:65
  551.0 11.7 %convolution_convert_fusion.2 = bf16[2,2048,896]{2,1,0:T(8,128)(2,1)} fusion(bf16[2,768,2048]{2,1,0:T(8,128)(2,1)} %bitcast.28, bf16[2,768,896]{2,1,0:T(8,128)(2,1)} %all-gather.12.cloned.1.call-done), kind=kOutput, calls=%fused_computation.10 | convolution fusion | flops 5640814592 | bytes 16384000 | tf_op jit(solution)/shard_map/erd,erf->edf/dot_general | solution.py:70
  562.7 8.9 %convolution_convert_fusion.1 = bf16[2,2048,896]{2,1,0:T(8,128)(2,1)} fusion(bf16[2,768,2048]{2,1,0:T(8,128)(2,1)S(1)} %bitcast.31, bf16[2,768,896]{2,1,0:T(8,128)(2,1)S(1)} %copy-done.4), kind=kOutput, calls=%fused_computation.9 | convolution fusion | flops 5640814592 | bytes 16384000 | tf_op jit(solution)/shard_map/erd,erf->edf/dot_general | solution.py:73
  571.7 8.2 convolution_convert_fusion
  579.8 110.0 %reduce-scatter.10.cloned.1.call-done = f32[128,2048]{1,0:T(8,128)} async-done(((f32[2048,2048]{1,0:T(8,128)}), f32[128,2048]{1,0:T(8,128)}) %reduce-scatter.10.cloned.1.call-update) | async-done | bytes 1048592 | tf_op jit(solution)/shard_map/reduce_scatter | solution.py:46
  689.8 2.1 convert_element_type.25
  691.9 180.0 %reduce-scatter.14.cloned.1.call-done = f32[128,2048]{1,0:T(8,128)} async-done(((f32[2048,2048]{1,0:T(8,128)}), f32[128,2048]{1,0:T(8,128)}) %reduce-scatter.14.cloned.1.call-update) | async-done | bytes 1048592 | tf_op jit(solution)/shard_map/reduce_scatter | solution.py:67
  871.9 2.1 convert_element_type.28
  (40 shorter events, 1.0 us)
Async XLA Ops:
  7.2 198.9 %copy-start = (f32[2,768]{1,0:T(2,128)S(1)}, f32[2,768]{1,0:T(2,128)}, u32[]{:S(2)}) copy-start(f32[2,768]{1,0:T(2,128)} %param.9) | copy-start | bytes 18436
  7.2 80.6 %all-gather.6.cloned.1.call-start = ((), (), s32[]{:S(2)}) async-start(), calls=%async_computation.5 | async-start | bytes 8912896 | tf_op jit(solution)/shard_map/all_gather | solution.py:24
  7.9 155.2 %all-gather.10.cloned.1.call-start = ((), (), s32[]{:S(2)}) async-start(), calls=%async_computation.10 | async-start | bytes 8912896 | tf_op jit(solution)/shard_map/all_gather | solution.py:49
  8.7 224.2 %reduce-scatter.6.cloned.1.call-start = ((), (), s32[]{:S(2)}) async-start(), calls=%async_computation.6 | async-start | bytes 8257536 | tf_op jit(solution)/shard_map/reduce_scatter | solution.py:32
  117.4 186.8 %reduce-scatter.12.cloned.1.call-start = ((), (), s32[]{:S(2)}) async-start(), calls=%async_computation.11 | async-start | bytes 8257536 | tf_op jit(solution)/shard_map/reduce_scatter | solution.py:52
  193.2 181.8 %reduce-scatter.8.cloned.1.call-start = ((), (), s32[]{:S(2)}) async-start(), calls=%async_computation.7 | async-start | bytes 8257536 | tf_op jit(solution)/shard_map/reduce_scatter | solution.py:33
  206.0 215.1 %all-gather.8.cloned.1.call-start = ((), (), s32[]{:S(2)}) async-start(), calls=%async_computation.8 | async-start | bytes 4128768 | tf_op jit(solution)/shard_map/all_gather | solution.py:39
  206.1 176.1 %copy-start.2 = (s32[2,768]{1,0:T(2,128)S(1)}, s32[2,768]{1,0:T(2,128)}, u32[]{:S(2)}) copy-start(s32[2,768]{1,0:T(2,128)} %param.8) | copy-start | bytes 18436
  380.5 83.4 %all-gather.12.cloned.1.call-start = ((), (), s32[]{:S(2)}) async-start(), calls=%async_computation.12 | async-start | bytes 4128768 | tf_op jit(solution)/shard_map/all_gather | solution.py:55
  381.2 125.4 %all-gather.14.cloned.1.call-start = ((), (), s32[]{:S(2)}) async-start(), calls=%async_computation.13 | async-start | bytes 4128768 | tf_op jit(solution)/shard_map/all_gather | solution.py:56
  382.0 307.9 %reduce-scatter.10.cloned.1.call-start = ((), (), s32[]{:S(2)}) async-start(), calls=%async_computation.9 | async-start | bytes 17825792 | tf_op jit(solution)/shard_map/reduce_scatter | solution.py:46
  461.2 410.7 %reduce-scatter.14.cloned.1.call-start = ((), (), s32[]{:S(2)}) async-start(), calls=%async_computation.14 | async-start | bytes 17825792 | tf_op jit(solution)/shard_map/reduce_scatter | solution.py:67
  551.0 11.7 %slice-start = ((s8[6291456]{0:T(1024)(128)(4,1)}), s8[2097152]{0:T(1024)(128)(4,1)S(1)}, s32[]{:S(2)}) async-start(s8[6291456]{0:T(1024)(128)(4,1)} %bitcast.29), calls=%async_computation.15 | async-start | bytes 4194304
  551.0 11.7 %slice-start.1 = ((s8[6291456]{0:T(1024)(128)(4,1)}), s8[4194304]{0:T(1024)(128)(4,1)S(1)}, s32[]{:S(2)}) async-start(s8[6291456]{0:T(1024)(128)(4,1)} %bitcast.29), calls=%async_computation.16 | async-start | bytes 8388608
  551.0 11.7 %copy-start.4 = (bf16[2,768,896]{2,1,0:T(8,128)(2,1)S(1)}, bf16[2,768,896]{2,1,0:T(8,128)(2,1)}, u32[]{:S(2)}) copy-start(bf16[2,768,896]{2,1,0:T(8,128)(2,1)} %all-gather.14.cloned.1.call-done) | copy-start | bytes 8257540
  551.0 20.6 %slice-start.2 = ((s8[6291456]{0:T(1024)(128)(4,1)}), s8[4194304]{0:T(1024)(128)(4,1)S(1)}, s32[]{:S(2)}) async-start(s8[6291456]{0:T(1024)(128)(4,1)} %bitcast.33), calls=%async_computation.17 | async-start | bytes 8388608
  562.7 8.9 %slice-start.3 = ((s8[6291456]{0:T(1024)(128)(4,1)}), s8[2097152]{0:T(1024)(128)(4,1)S(1)}, s32[]{:S(2)}) async-start(s8[6291456]{0:T(1024)(128)(4,1)} %bitcast.33), calls=%async_computation.18 | async-start | bytes 4194304
  562.7 8.9 %copy-start.3 = (bf16[2,768,896]{2,1,0:T(8,128)(2,1)S(1)}, bf16[2,768,896]{2,1,0:T(8,128)(2,1)}, u32[]{:S(2)}) copy-start(bf16[2,768,896]{2,1,0:T(8,128)(2,1)} %all-gather.8.cloned.1.call-done) | copy-start | bytes 8257540
  571.7 302.3 %copy-start.1 = (f32[2,768]{1,0:T(2,128)S(1)}, f32[2,768]{1,0:T(2,128)}, u32[]{:S(2)}) copy-start(f32[2,768]{1,0:T(2,128)} %param.9) | copy-start | bytes 18436
Sparse Core Ops, SparseCore 0:
  10.2 77.5 all-gather.5
  90.0 73.1 all-gather.9
  166.0 66.7 reduce-scatter.5
  235.7 68.5 reduce-scatter.11
  306.4 68.5 reduce-scatter.7
  380.6 40.5 all-gather.7
  423.3 40.4 all-gather.11
  466.1 40.4 all-gather.13
  511.3 178.5 reduce-scatter.9
  694.4 177.4 reduce-scatter.13
where the time goes:
time: 886 us; the launch traced here: 881 us
  waiting for transfers between devices  657 us (74%)
  matrix products  107 us (12%)
  other arithmetic  67.3 us (8%)
  local copies, waits for them, and re-layouts  34.4 us (4%)
  between operations  14.8 us (2%)
    reduce_scatter x1, waiting for transfers between devices, local(): lax.psum_scatter(grad_buffer, 'loop', scatter_dimension=0, tiled=True)  180 us
    reduce_scatter x1, waiting for transfers between devices, local(): lax.psum_scatter(out_buffer, 'loop', scatter_dimension=0, tiled=True)  110 us
    all_gather x1, waiting for transfers between devices, local(): everyone = lax.all_gather(features, 'loop', axis=0, tiled=True)  78.4 us
    reduce_scatter x1, waiting for transfers between devices, local(): lax.psum_scatter(back_part, 'tok', scatter_dimension=1, tiled=True)  71.4 us
    reduce_scatter x1, waiting for transfers between devices, local(): lax.psum_scatter(up_part, 'tok', scatter_dimension=1, tiled=True)  70.7 us
    all_gather x1, waiting for transfers between devices, local(): grad_everyone = lax.all_gather(out_grad, 'loop', axis=0, tiled=True)  45.2 us
    all_gather x1, waiting for transfers between devices, local(): scaled = lax.all_gather(scaled_share, 'tok', axis=1, tiled=True)  38.9 us
    all_gather x1, waiting for transfers between devices, local(): lax.all_gather(up_bar_share, 'tok', axis=1, tiled=True)  30.3 us
  transfers between devices with their start and end apart: 10, of which 10 were waited for; matrix products, arithmetic and copies ran while one was open for 23% of the time, Pallas kernels for 0%

commit v1 on v0

v1 whole, which is shorter than its diff:
```python
import functools

import jax
import jax.numpy as jnp
import numpy as np
from jax import lax
from jax.experimental import pallas as pl
from jax.experimental.pallas import tpu as pltpu
from jax.sharding import PartitionSpec as P

BF16 = jnp.bfloat16
F32 = jnp.float32
VMEM_LIMIT = 56 * 1024 * 1024
ROW_TILE = 256
TOKEN_TILE = 256
HIDDEN_TILE = 256


ORDER = (
    ("pick", "token", 0),
    ("part", "gate", 0),
    ("part", "up", 0),
    ("pick", "token", 1),
    ("pair", 1),
    ("pick", "grad", 0),
    ("part", "back", 0),
    ("hidden", "mixed", 0),
    ("pick", "grad", 1),
    ("part", "back", 1),
    ("weigh", "down", 0),
    ("hidden", "mixed", 1),
    ("weigh", "down", 1),
    ("across", "mixed"),
    ("hidden", "grad", 0),
    ("onward", "mixed", 0),
    ("weigh", "gate", 0),
    ("onward", "mixed", 1),
    ("weigh", "up", 0),
    ("hidden", "grad", 1),
    ("finish", "mixed"),
    ("across", "grad"),
    ("weigh", "gate", 1),
    ("onward", "grad", 0),
    ("weigh", "up", 1),
    ("onward", "grad", 1),
    ("finish", "grad"),
)


COST = pl.CostEstimate(flops=40_000_000_000, bytes_accessed=1024, transcendentals=0)


def params():
    return pltpu.CompilerParams(vmem_limit_bytes=VMEM_LIMIT)


def resident(shape, index):
    return pl.BlockSpec(shape, index, pipeline_mode=pl.Buffered(1))


def after_specs(after):
    return [pl.BlockSpec(memory_space=pl.ANY)] * len(after)


def pair_kernel(a_ref, gate_ref, up_ref, *refs):
    wide_ref, sent_ref = refs[-2:]

    def product(weight_ref):
        out = jnp.dot(a_ref[...], weight_ref[...], preferred_element_type=F32)
        wide_ref[...] = out
        sent_ref[...] = out.astype(BF16)

    pl.when(pl.program_id(1) == 0)(lambda: product(gate_ref))
    pl.when(pl.program_id(1) == 1)(lambda: product(up_ref))


def pair_product(rows, gate, up, expert, after):
    count, depth = rows.shape
    hidden = gate.shape[2]
    tile = count // 3
    weight_spec = resident((None, depth, hidden), lambda i, j: (expert, 0, 0))
    return pl.pallas_call(
        pair_kernel,
        grid=(3, 2),
        in_specs=[pl.BlockSpec((tile, depth), lambda i, j: (i, 0)), weight_spec, weight_spec]
        + after_specs(after),
        out_specs=[pl.BlockSpec((None, tile, hidden), lambda i, j: (j, i, 0))] * 2,
        out_shape=[
            jax.ShapeDtypeStruct((2, count, hidden), F32),
            jax.ShapeDtypeStruct((2, count, hidden), BF16),
        ],
        compiler_params=params(),
        cost_estimate=COST,
    )(rows, gate, up, *after)


def order_kernel(block, column_ref, line_ref, weight_ref, rows_out, weights_out, both_out):
    def keys(tokens, both, expert):
        late = both if expert == 0 else 1.0 - both
        held = lax.div(tokens, block)
        return (held * 2 * block + (tokens - held * block)).astype(F32) + late * block

    for e in range(2):
        column, line = column_ref[e], line_ref[e]
        both_column = jnp.max((column == line_ref[1 - e]).astype(F32), axis=1, keepdims=True)
        both_line = jnp.max((line == column_ref[1 - e]).astype(F32), axis=0, keepdims=True)
        before = keys(column, both_column, e) < keys(line, both_line, e)
        place = jnp.sum(before.astype(F32), axis=0, keepdims=True)
        spot = lax.broadcasted_iota(jnp.int32, column.shape, 0).astype(F32)
        chosen = (place == spot).astype(F32)
        rows = jnp.sum(chosen * line.astype(F32), axis=1, keepdims=True)
        rows_out[e] = rows.astype(jnp.int32)
        weights_out[e] = jnp.sum(chosen * weight_ref[e], axis=1, keepdims=True)
        both_out[e] = both_line


def order_rows(expert_rows, route_weight, block):
    experts, count = expert_rows.shape
    return pl.pallas_call(
        functools.partial(order_kernel, block),
        out_shape=[
            jax.ShapeDtypeStruct((experts, count, 1), jnp.int32),
            jax.ShapeDtypeStruct((experts, count, 1), F32),
            jax.ShapeDtypeStruct((experts, 1, count), F32),
        ],
        compiler_params=params(),
    )(expert_rows[:, :, None], expert_rows[:, None, :], route_weight[:, None, :])


def pick_kernel(first_ref, last_ref, rows_ref, table_ref, *refs):
    out_ref, acc = refs[-2:]
    i = pl.program_id(0)
    rows = rows_ref[...]
    acc[...] = jnp.zeros_like(acc)
    lane = lax.broadcasted_iota(jnp.int32, (rows.shape[0], TOKEN_TILE), 1)

    def step(b, carry):
        base = pl.multiple_of(b * TOKEN_TILE, TOKEN_TILE)
        hot = (lane + base == rows).astype(F32).astype(BF16)
        acc[...] += jnp.dot(
            hot, table_ref[pl.ds(base, TOKEN_TILE), :], preferred_element_type=F32
        )
        return carry

    lax.fori_loop(first_ref[i], last_ref[i] + 1, step, 0)
    out_ref[...] = acc[...].astype(BF16)


def pick_rows(table, rows, after):
    count = rows.shape[0]
    tokens, width = table.shape
    tiles = count // ROW_TILE
    tiled = rows.reshape(tiles, ROW_TILE) // TOKEN_TILE
    return pl.pallas_call(
        pick_kernel,
        grid_spec=pltpu.PrefetchScalarGridSpec(
            num_scalar_prefetch=2,
            grid=(tiles,),
            in_specs=[
                pl.BlockSpec((ROW_TILE, 1), lambda i, *_: (i, 0)),
                resident((tokens, width), lambda i, *_: (0, 0)),
            ]
            + after_specs(after),
            out_specs=pl.BlockSpec((ROW_TILE, width), lambda i, *_: (i, 0)),
            scratch_shapes=[pltpu.VMEM((ROW_TILE, width), F32)],
        ),
        out_shape=jax.ShapeDtypeStruct((count, width), BF16),
        compiler_params=params(),
        cost_estimate=COST,
    )(tiled[:, 0], tiled[:, -1], rows, table, *after)


def part_kernel(flip, a_ref, w_ref, *refs):
    wide_ref, sent_ref = refs[-2:]
    dims = (((1,), (1 if flip else 0,)), ((), ()))
    out = lax.dot_general(a_ref[...], w_ref[...], dims, preferred_element_type=F32)
    wide_ref[...] = out
    sent_ref[...] = out.astype(BF16)


def partial_product(rows, weight, expert, flip, after):
    count, depth = rows.shape
    hidden = weight.shape[1] if flip else weight.shape[2]
    tile = count // 3
    return pl.pallas_call(
        functools.partial(part_kernel, flip),
        grid=(3,),
        in_specs=[
            pl.BlockSpec((tile, depth), lambda i: (i, 0)),
            resident((None,) + weight.shape[1:], lambda i: (expert, 0, 0)),
        ]
        + after_specs(after),
        out_specs=[
            pl.BlockSpec((tile, hidden), lambda i: (i, 0)),
            pl.BlockSpec((tile, hidden), lambda i: (i, 0)),
        ],
        out_shape=[
            jax.ShapeDtypeStruct((count, hidden), F32),
            jax.ShapeDtypeStruct((count, hidden), BF16),
        ],
        compiler_params=params(),
        cost_estimate=COST,
    )(rows, weight, *after)


def hidden_kernel(backward, cap, layout_ref, weight_ref, *refs):
    shares = 6 if backward else 4
    terms = 2 if backward else 1
    parts, rights = refs[:shares], refs[shares : shares + terms]
    merge = layout_ref is not None
    first, acc = (refs[shares + terms], refs[-1]) if merge else (None, None)
    outs = refs[-(5 + terms) : -1] if merge else refs[-(1 + terms) :]
    lefts, results = outs[:terms], outs[terms:]
    count = lefts[0].shape[0]
    step = pl.program_id(0)
    chunks = count // HIDDEN_TILE

    @pl.when(step < chunks)
    def _():
        at = pl.ds(pl.multiple_of(step * HIDDEN_TILE, HIDDEN_TILE), HIDDEN_TILE)
        gate = parts[0][...] + parts[1][...].astype(F32)
        upval = parts[2][...] + parts[3][...].astype(F32)
        weights = weight_ref[...]
        sigma = jax.nn.sigmoid(gate)
        if backward:
            weighted = weights * (parts[4][...] + parts[5][...].astype(F32))
            gate_bar = weighted * upval * sigma * (1.0 + gate * (1.0 - sigma))
            lefts[0][at, :] = gate_bar.astype(BF16)
            lefts[1][at, :] = (weighted * gate * sigma).astype(BF16)
        else:
            lefts[0][at, :] = (weights * (gate * sigma) * upval).astype(BF16)

    @pl.when(step >= chunks)
    def _():
        dims = (((1,), (1 if backward else 0,)), ((), ()))
        total = None
        for left, right in zip(lefts, rights):
            term = lax.dot_general(left[...], right[...], dims, preferred_element_type=F32)
            total = term if total is None else total + term
        if not merge:
            results[0][pl.ds(0, count), :] = total
            return
        blocks, block = results[0].shape[:2]
        acc[pl.ds(block, count), :] = total
        slot = lax.broadcasted_iota(jnp.int32, (block, total.shape[1]), 0)
        near = slot[:cap]

        def run(ref, start, length):
            base = pl.multiple_of((start // 8) * 8, 8)
            window = ref[pl.ds(base, length + 8), :]
            return pltpu.roll(window, length + 8 - (start - base), 0)[:length]

        for which in range(4):
            for z in range(blocks):
                start0, count0, start1, lead, count1 = (
                    layout_ref[i, which * blocks + z] for i in range(5)
                )
                rows1 = run(acc, block + start1 - lead, block)
                rows1 = jnp.where((slot >= lead) & (slot < lead + count1), rows1, 0.0)
                rows0 = jnp.where(near < count0, run(first, start0, cap), 0.0)
                results[which][z, pl.ds(0, cap), :] = (rows0 + rows1[:cap]).astype(BF16)
                results[which][z, pl.ds(cap, block - cap), :] = rows1[cap:].astype(BF16)


def hidden_rows(backward, weights, shares, rights, expert, first, layout, block, cap, after):
    places = [place for _, place in shares]
    shares = [share for share, _ in shares]
    count, hidden = shares[0].shape[-2:]
    width = rights[0].shape[1] if backward else rights[0].shape[2]
    tile = min(512, width)
    terms = len(rights)
    chunks = count // HIDDEN_TILE
    padded = count + cap + 16

    def early(i, *_):
        return (jnp.minimum(i, chunks - 1), 0)

    def late(i):
        return jnp.maximum(i - chunks, 0)

    if backward:
        right_spec = pl.BlockSpec((None, tile, hidden), lambda i, *_: (expert, late(i), 0))
    else:
        right_spec = pl.BlockSpec((None, hidden, tile), lambda i, *_: (expert, 0, late(i)))
    rows_spec = pl.BlockSpec((padded, tile), lambda i, *_: (0, late(i)))
    in_specs = [pl.BlockSpec((HIDDEN_TILE, 1), early)]
    for place in places:
        if place is None:
            in_specs.append(pl.BlockSpec((HIDDEN_TILE, hidden), early))
        else:
            index = functools.partial(lambda place, i, *_: (place,) + early(i), place)
            in_specs.append(pl.BlockSpec((None, HIDDEN_TILE, hidden), index))
    in_specs += [right_spec] * terms
    out_specs = [resident((count, hidden), lambda i, *_: (0, 0))] * terms
    out_shape = [jax.ShapeDtypeStruct((count, hidden), BF16)] * terms
    kernel = functools.partial(hidden_kernel, backward, cap)
    if first is None:
        out_specs += [rows_spec]
        out_shape += [jax.ShapeDtypeStruct((padded, width), F32)]
        kernel = functools.partial(kernel, None)
        scratch, extra, scalars = [], [], []
    else:
        blocks = layout.shape[1] // 4
        in_specs += [rows_spec]
        out_specs += [pl.BlockSpec((blocks, block, tile), lambda i, *_: (0, 0, late(i)))] * 4
        out_shape += [jax.ShapeDtypeStruct((blocks, block, width), BF16)] * 4
        scratch = [pltpu.VMEM((block + count + block + 8, tile), F32)]
        extra, scalars = [first], [layout]
    outs = pl.pallas_call(
        kernel,
        grid_spec=pltpu.PrefetchScalarGridSpec(
            num_scalar_prefetch=len(scalars),
            grid=(chunks + width // tile,),
            in_specs=in_specs + after_specs(after),
            out_specs=out_specs,
            scratch_shapes=scratch,
        ),
        out_shape=out_shape,
        compiler_params=params(),
        cost_estimate=COST,
    )(*scalars, weights, *shares, *rights, *extra, *after)
    return outs[:terms], outs[terms:]


def grad_kernel(left_ref, right_ref, *refs):
    refs[-1][...] = lax.dot_general(
        left_ref[...], right_ref[...], (((0,), (0,)), ((), ())), preferred_element_type=F32
    ).astype(BF16)


def weight_grad(left, right, expert, experts, earlier, after):
    count, rows = left.shape
    columns = right.shape[1]
    tile = next(t for t in (512, 448, 128, rows) if rows % t == 0 and (t % 128 == 0 or t == rows))
    extra = ([] if earlier is None else [earlier]) + list(after)
    return pl.pallas_call(
        grad_kernel,
        grid=(rows // tile,),
        in_specs=[
            pl.BlockSpec((count, tile), lambda i: (0, i)),
            resident((count, columns), lambda i: (0, 0)),
        ]
        + after_specs(extra),
        out_specs=pl.BlockSpec((None, tile, columns), lambda i: (expert, i, 0)),
        out_shape=jax.ShapeDtypeStruct((experts, rows, columns), BF16),
        input_output_aliases={} if earlier is None else {2: 0},
        compiler_params=params(),
        cost_estimate=COST,
    )(left, right, *extra)


class Ring:
    def __init__(self, size):
        self.size = size
        self.depth = size // 4
        self.index = lax.axis_index("loop")
        self.z = self.index // 4
        self.x = (self.index // 2) % 2
        self.core = self.index % 2

    def send(self, value, dz=0, flip_x=False, flip_core=False):
        pairs = []
        for i in range(self.size):
            z, x, c = i // 4, (i // 2) % 2, i % 2
            z = (z + dz) % self.depth
            pairs.append((i, (z * 2 + (x ^ flip_x)) * 2 + (c ^ flip_core)))
        return lax.ppermute(value, "loop", pairs)

    def owners(self):
        z = (self.z + 1 + np.arange(self.depth)) % self.depth
        return jnp.concatenate(
            [(z * 2 + (self.x ^ x)) * 2 + (self.core ^ c) for c in (0, 1) for x in (0, 1)]
        )


def sum_kernel(sums, stacks, *refs):
    ins, outs = refs[:stacks], refs[-len(sums) :]
    for out, blocks in zip(outs, sums):
        for place, terms in enumerate(blocks):
            total = None
            for which, index in terms:
                term = ins[which][index].astype(F32)
                total = term if total is None else total + term
            out[place] = total.astype(BF16)


def sum_blocks(stacks, sums, after):
    rows, width = stacks[0].shape[1:]
    tile = min(1024, width)

    def spec(blocks):
        return pl.BlockSpec((blocks, rows, tile), lambda i: (0, 0, i))

    return pl.pallas_call(
        functools.partial(sum_kernel, sums, len(stacks)),
        grid=(width // tile,),
        in_specs=[spec(t.shape[0]) for t in stacks] + after_specs(after),
        out_specs=[spec(len(blocks)) for blocks in sums],
        out_shape=[jax.ShapeDtypeStruct((len(blocks), rows, width), BF16) for blocks in sums],
        compiler_params=params(),
        cost_estimate=COST,
    )(*stacks, *after)


def place_kernel(terms, hot_ref, *refs):
    total = None
    for ref in refs[:terms]:
        term = ref[0].astype(F32)
        total = term if total is None else total + term
    out = jnp.dot(
        hot_ref[...], total, precision=lax.Precision.HIGHEST, preferred_element_type=F32
    )
    refs[-1][...] = out.astype(BF16)


def place_slots(hot, stacks, after):
    block = hot.shape[0]
    width = stacks[0].shape[2]
    tile = min(512, width)
    specs = [
        pl.BlockSpec((1, block, tile), functools.partial(lambda last, i: (last, 0, i), t.shape[0] - 1))
        for t in stacks
    ]
    return pl.pallas_call(
        functools.partial(place_kernel, len(stacks)),
        grid=(width // tile,),
        in_specs=[pl.BlockSpec((block, block), lambda i: (0, 0))] + specs + after_specs(after),
        out_specs=pl.BlockSpec((block, tile), lambda i: (0, i)),
        out_shape=jax.ShapeDtypeStruct((block, width), BF16),
        compiler_params=params(),
        cost_estimate=COST,
    )(hot, *stacks, *after)


class Reduction:
    def __init__(self, ring, held):
        self.ring, self.held = ring, held
        self.got_far = ring.send(held[3], flip_core=True)
        self.got_near = ring.send(held[2], flip_core=True)
        depth = ring.depth
        turns = sorted(range(1, depth), key=lambda k: (-min(k, depth - k), k))
        cut = max(1, (depth - 1) // 3)
        self.groups = [turns[:cut], turns[cut:], [depth]]

    def across(self, after):
        sums = [[[(0, k - 1), (1, k - 1)] for k in group] for group in self.groups]
        values = sum_blocks([self.held[1], self.got_far], sums, after)
        self.from_x = [self.ring.send(value, flip_x=True) for value in values]
        self.along = []
        return values[0]

    def onward(self, turn, after):
        group = self.groups[turn]
        sums = [[[(0, k - 1), (1, k - 1), (2, place)]] for place, k in enumerate(group)]
        values = sum_blocks([self.held[0], self.got_near, self.from_x[turn]], sums, after)
        self.along += [self.ring.send(value, dz=k) for value, k in zip(values, group)]
        return values[0]

    def finish(self, hot, after):
        stacks = [self.held[0], self.got_near, self.from_x[2]] + self.along
        return place_slots(hot, stacks, after)


def over_tok(wide, sent):
    if lax.axis_size("tok") == 2:
        return [wide, lax.ppermute(sent, "tok", [(0, 1), (1, 0)])]
    return [lax.psum(wide, "tok"), jnp.zeros_like(sent)]


def local(features, expert_rows, route_weight, gate_proj, up_proj, down_proj, out_grad):
    loop_size = lax.axis_size("loop")
    ring = Ring(loop_size)
    block = features.shape[0]
    experts, rows_each = expert_rows.shape
    cap = 2 * rows_each // loop_size
    token_table = lax.all_gather(features, "loop", axis=0, tiled=True)
    grad_table = lax.all_gather(out_grad, "loop", axis=0, tiled=True)

    ordered, weights, both = order_rows(expert_rows, route_weight, block)
    edges = jnp.arange(loop_size + 1, dtype=jnp.int32) * block
    bounds = jnp.sum((expert_rows[:, None, :] < edges[None, :, None]).astype(jnp.int32), axis=2)
    starts, counts = bounds[:, :-1], bounds[:, 1:] - bounds[:, :-1]
    alone = (both[0, 0] < 0.5) & (expert_rows[0] // block == jnp.arange(loop_size)[:, None])
    lead = jnp.sum(alone.astype(jnp.int32), axis=1)
    layout = jnp.stack([starts[0], counts[0], starts[1], lead, counts[1]])
    start0, count0, start1, first1, count1 = jnp.take(layout, ring.index, axis=1)
    layout = jnp.take(layout, ring.owners(), axis=1)
    slot = jnp.arange(block, dtype=jnp.int32)

    def token_at(e, row):
        return jnp.take(ordered[e, :, 0], jnp.clip(row, 0, rows_each - 1))

    late = (slot >= first1) & (slot < first1 + count1)
    token = jnp.where(late, token_at(1, start1 + slot - first1), -1)
    token = jnp.where(slot < count0, token_at(0, start0 + slot), token)
    hot = (ring.index * block + slot)[:, None] == token[None, :]
    hot = hot.astype(F32)

    rows = {"token": [None, None], "grad": [None, None]}
    shares = {"gate": [None, None], "up": [None, None], "back": [None, None]}
    lefts = {"mixed": [None, None], "grad": [None, None]}
    first, sums, placed = {}, {}, {}
    grads = {"gate": None, "up": None, "down": None}
    last = []

    def pick(which, e):
        table = token_table if which == "token" else grad_table
        rows[which][e] = pick_rows(table, ordered[e], last)
        return rows[which][e]

    def part(which, e):
        source = rows["grad" if which == "back" else "token"][e]
        weight = {"gate": gate_proj, "up": up_proj, "back": down_proj}[which]
        share = partial_product(source, weight, e, which == "back", last)
        shares[which][e] = [(value, None) for value in over_tok(*share)]
        return share[0]

    def pair(e):
        share = pair_product(rows["token"][e], gate_proj, up_proj, e, last)
        both_shares = over_tok(*share)
        for place, which in enumerate(("gate", "up")):
            shares[which][e] = [(value, place) for value in both_shares]
        return share[0]

    def hidden(which, e):
        backward = which == "grad"
        parts = shares["gate"][e] + shares["up"][e] + (shares["back"][e] if backward else [])
        rights = [gate_proj, up_proj] if backward else [down_proj]
        lefts[which][e], results = hidden_rows(
            backward, weights[e], parts, rights, e, first.get(which), layout, block, cap, last
        )
        if e:
            sums[which] = Reduction(ring, results)
        else:
            first[which] = results[0]
        return lefts[which][e][0]

    def across(which):
        return sums[which].across(last)

    def onward(which, turn):
        return sums[which].onward(turn, last)

    def finish(which):
        placed[which] = sums[which].finish(hot, last)
        return placed[which]

    def weigh(which, e):
        if which == "down":
            left, right = lefts["mixed"][e][0], rows["grad"][e]
        else:
            left, right = rows["token"][e], lefts["grad"][e][0 if which == "gate" else 1]
        grads[which] = weight_grad(left, right, e, experts, grads[which], last)
        return grads[which]

    steps = {
        "pick": pick,
        "part": part,
        "pair": pair,
        "hidden": hidden,
        "across": across,
        "onward": onward,
        "finish": finish,
        "weigh": weigh,
    }
    for step, *detail in ORDER:
        last = [steps[step](*detail)]
    return (placed["mixed"], placed["grad"], grads["gate"], grads["up"], grads["down"])


def solution(mesh):
    placed = (
        P("loop", "tok"),
        P(),
        P(),
        P(None, "tok", "loop"),
        P(None, "tok", "loop"),
        P(None, "loop", "tok"),
        P("loop", "tok"),
    )
    return jax.shard_map(
        local,
        mesh=mesh,
        in_specs=placed,
        out_specs=(
            P("loop", "tok"),
            P("loop", "tok"),
            P(None, "tok", "loop"),
            P(None, "tok", "loop"),
            P(None, "loop", "tok"),
        ),
        check_vma=False,
    )
```

time: 886 us -> 447 us (0.50)
  waiting for transfers between devices: 657 us -> 130 us
  Pallas kernels: 0 us -> 249 us
  matrix products: 107 us -> 0 us
  other arithmetic: 67.3 us -> 7.26 us
  starting transfers between devices: 1.25 us -> 21.3 us
  local copies, waits for them, and re-layouts: 34.4 us -> 21.7 us
    reduce_scatter x5 -> x0, waiting for transfers between devices: 459 us -> none  [the longest x1 180 us: local(): lax.psum_scatter(grad_buffer, 'loop', scatter_dimension=0, tiled=True)]
    pallas_call x0 -> x28, Pallas kernels: none -> 249 us  [the longest x4 82.7 us: hidden_rows(): pl.pallas_call(kernel, grid_spec=pltpu.PrefetchScalarGridSpec(num_scalar_...]
    all_gather x5 -> x2, waiting for transfers between devices: 195 us -> 74.4 us  [the longest x1 52.6 us: local(): token_table = lax.all_gather(features, 'loop', axis=0, tiled=True)]
    dot_general x9 -> x0, matrix products: 107 us -> none  [the longest x1 15.1 us: local(): jnp.einsum('erf,edf->erd', up_bar, up_proj, preferred_element_type=jnp.fl...]
    scatter-add x2 -> x0, other arithmetic: 56.9 us -> none  [the longest x1 29.2 us: local(): grad_buffer = jnp.zeros((total_tokens, width), jnp.float32).at[flat_rows]...]
    ppermute x0 -> x21, waiting for transfers between devices: none -> 54.5 us  [the longest x16 40.9 us: send(): return lax.ppermute(value, 'loop', pairs)]
    gather x2 -> x4, local copies, waits for them, and re-layouts: 34.3 us -> 2.78 us  [the longest x2 2.12 us: token_at(): return jnp.take(ordered[e, :, 0], jnp.clip(row, 0, rows_each - 1))]
    ppermute x0 -> x21, starting transfers between devices: none -> 21.3 us  [the longest x16 15.7 us: send(): return lax.ppermute(value, 'loop', pairs)]
  transfers between devices with their start and end apart: 10 -> 23, of which waited for: 10 -> 9; matrix products, arithmetic and copies ran while one was open for 23% -> 4% of each run, Pallas kernels for 0% -> 55%
where the time goes in v1:
time: 447 us; the launch traced here: 446 us
  Pallas kernels  249 us (56%)
  waiting for transfers between devices  130 us (29%)
  local copies, waits for them, and re-layouts  21.7 us (5%)
  starting transfers between devices  21.3 us (5%)
  between operations  15.6 us (3%)
  other arithmetic  7.26 us (2%)
    pallas_call x4, Pallas kernels, hidden_rows(): pl.pallas_call(kernel, grid_spec=pltpu.PrefetchScalarGridSpec(num_scalar_...  82.7 us
    all_gather x1, waiting for transfers between devices, local(): token_table = lax.all_gather(features, 'loop', axis=0, tiled=True)  52.6 us
    pallas_call x6, Pallas kernels, weight_grad(): pl.pallas_call(grad_kernel, grid=(rows // tile,), in_specs=[pl.BlockSpec(...  45.7 us
    pallas_call x4, Pallas kernels, pick_rows(): pl.pallas_call(pick_kernel, grid_spec=pltpu.PrefetchScalarGridSpec(num_sc...  42.7 us
    ppermute x16, waiting for transfers between devices, send(): return lax.ppermute(value, 'loop', pairs)  40.9 us
    pallas_call x4, Pallas kernels, partial_product(): pl.pallas_call(functools.partial(part_kernel, flip), grid=(3,), in_specs=...  31 us
    all_gather x1, waiting for transfers between devices, local(): grad_table = lax.all_gather(out_grad, 'loop', axis=0, tiled=True)  21.8 us
    pallas_call x6, Pallas kernels, sum_blocks(): pl.pallas_call(functools.partial(sum_kernel, sums, len(stacks)), grid=(wi...  19.6 us
  transfers between devices with their start and end apart: 23, of which 9 were waited for; matrix products, arithmetic and copies ran while one was open for 4% of the time, Pallas kernels for 55%

profile of v1, /device:TPU:0, one launch (start us, length us, event | category | flops | bytes accessed | tf_op | source)
XLA Modules:
  0.0 445.6 jit_solution(10769663246032076419)
XLA Ops:
  13.9 5.1 %shard_map.119 = (s32[2,768,1]{2,1,0:T(8,128)}, f32[2,768,1]{2,1,0:T(8,128)}, f32[2,1,768]{2,1,0:T(1,128)}) custom-call(s32[2,768,1]{2,1,0:T(8,128)} %copy.32.column_ref, s32[2,1,768]{2,1,0:T(1,128)} %broadcast_in_dim.47.line_ref, f32[2,1,768]{2,1,0:T(1,128)} %broadcast_in_dim.48.weight_ref), custom_call_target="tpu_custom_call" | custom-call | tf_op jit(solution)/shard_map/pallas_call | solution.py:119
  35.2 52.6 %all-gather.3.cloned.1.call-done.table_ref = bf16[2048,2048]{1,0:T(8,128)(2,1)} async-done(((bf16[128,2048]{1,0:T(8,128)(2,1)}), bf16[2048,2048]{1,0:T(8,128)(2,1)}) %all-gather.3.cloned.1.call-update) | async-done | bytes 8388624 | tf_op jit(solution)/shard_map/all_gather | solution.py:476
  87.8 10.7 %shard_map.120.a_ref.refs_0_.left_ref = bf16[768,2048]{1,0:T(8,128)(2,1)} custom-call(s32[3]{0:T(128)} %get-tuple-element.98.first_ref, s32[3]{0:T(128)} %get-tuple-element.97.last_ref, s32[768,1]{1,0:T(8,128)} %get-tuple-element.103.rows_ref, bf16[2048,2048]{1,0:T(8,128)(2,1)} %all-gather.3.cloned.1.call-done.table_ref), custom_call_target="tpu_custom_call" | custom-call | flops 40000000000 | bytes 1024 | tf_op jit(solution)/shard_map/pallas_call | solution.py:154
  98.5 7.7 %shard_map.121 = (f32[768,896]{1,0:T(8,128)}, bf16[768,896]{1,0:T(8,128)(2,1)}) custom-call(bf16[768,2048]{1,0:T(8,128)(2,1)} %shard_map.120.a_ref.refs_0_.left_ref, bf16[2,2048,896]{2,1,0:T(8,128)(2,1)} %refs_6_.3, bf16[768,2048]{1,0:T(8,128)(2,1)} %shard_map.120.a_ref.refs_0_.left_ref), custom_call_target="tpu_custom_call" | custom-call | flops 40000000000 | bytes 1024 | tf_op jit(solution)/shard_map/pallas_call | solution.py:185
  106.1 7.7 %shard_map.122 = (f32[768,896]{1,0:T(8,128)}, bf16[768,896]{1,0:T(8,128)(2,1)}) custom-call(bf16[768,2048]{1,0:T(8,128)(2,1)} %shard_map.120.a_ref.refs_0_.left_ref, bf16[2,2048,896]{2,1,0:T(8,128)(2,1)} %refs_7_.3, f32[768,896]{1,0:T(8,128)} %get-tuple-element.48.refs_0_), custom_call_target="tpu_custom_call" | custom-call | flops 40000000000 | bytes 1024 | tf_op jit(solution)/shard_map/pallas_call | solution.py:185
  115.9 10.7 %shard_map.123.a_ref.refs_0_.left_ref = bf16[768,2048]{1,0:T(8,128)(2,1)} custom-call(s32[3]{0:T(128)} %get-tuple-element.100.first_ref, s32[3]{0:T(128)} %get-tuple-element.99.last_ref, s32[768,1]{1,0:T(8,128)} %get-tuple-element.104.rows_ref, bf16[2048,2048]{1,0:T(8,128)(2,1)} %all-gather.3.cloned.1.call-done.table_ref, ...), custom_call_target="tpu_custom_call" | custom-call | flops 40000000000 | bytes 1024 | tf_op jit(solution)/shard_map/pallas_call | solution.py:154
  126.6 13.3 %shard_map.124 = (f32[2,768,896]{2,1,0:T(8,128)}, bf16[2,768,896]{2,1,0:T(8,128)(2,1)}) custom-call(bf16[768,2048]{1,0:T(8,128)(2,1)} %shard_map.123.a_ref.refs_0_.left_ref, bf16[2,2048,896]{2,1,0:T(8,128)(2,1)} %refs_6_.3, bf16[2,2048,896]{2,1,0:T(8,128)(2,1)} %refs_7_.3, bf16[768,2048]{1,0:T(8,128)(2,1)} %shard_map.123.a_ref.refs_0_.left_ref), custom_call_target="tpu_custom_call" | custom-call | flops 40000000000 | bytes 1024 | tf_op jit(solution)/shard_map/pallas_call | solution.py:82
  141.3 21.8 %all-gather.5.cloned.1.call-done.table_ref = bf16[2048,2048]{1,0:T(8,128)(2,1)} async-done(((bf16[128,2048]{1,0:T(8,128)(2,1)}), bf16[2048,2048]{1,0:T(8,128)(2,1)}) %all-gather.5.cloned.1.call-update) | async-done | bytes 8388624 | tf_op jit(solution)/shard_map/all_gather | solution.py:477
  163.1 10.7 %shard_map.125.a_ref.refs_0_.right_ref = bf16[768,2048]{1,0:T(8,128)(2,1)} custom-call(s32[3]{0:T(128)} %get-tuple-element.98.first_ref, s32[3]{0:T(128)} %get-tuple-element.97.last_ref, s32[768,1]{1,0:T(8,128)} %get-tuple-element.103.rows_ref, bf16[2048,2048]{1,0:T(8,128)(2,1)} %all-gather.5.cloned.1.call-done.table_ref, ...), custom_call_target="tpu_custom_call" | custom-call | flops 40000000000 | bytes 1024 | tf_op jit(solution)/shard_map/pallas_call | solution.py:154
  173.8 7.8 %shard_map.126 = (f32[768,896]{1,0:T(8,128)}, bf16[768,896]{1,0:T(8,128)(2,1)}) custom-call(bf16[768,2048]{1,0:T(8,128)(2,1)} %shard_map.125.a_ref.refs_0_.right_ref, bf16[2,896,2048]{2,1,0:T(8,128)(2,1)} %refs_4_.3, bf16[768,2048]{1,0:T(8,128)(2,1)} %shard_map.125.a_ref.refs_0_.right_ref), custom_call_target="tpu_custom_call" | custom-call | flops 40000000000 | bytes 1024 | tf_op jit(solution)/shard_map/pallas_call | solution.py:185
  183.0 11.3 %shard_map.127 = (bf16[768,896]{1,0:T(8,128)(2,1)}, f32[880,2048]{1,0:T(8,128)}) custom-call(f32[768,1]{1,0:T(8,128)} %get-tuple-element.101.weight_ref, f32[768,896]{1,0:T(8,128)} %get-tuple-element.48.refs_0_, bf16[768,896]{1,0:T(8,128)(2,1)} %collective-permute-done.1.refs_1_, f32[768,896]{1,0:T(8,128)} %get-tuple-element.49.refs_0_.refs_2_, ...), custom_call_target="tpu_custom_call" | custom-call | flops 40000000000 | bytes 1024 | tf_op jit(solution)/shard_map/pallas_call | solution.py:309
  194.4 10.7 %shard_map.128.a_ref.refs_0_.right_ref = bf16[768,2048]{1,0:T(8,128)(2,1)} custom-call(s32[3]{0:T(128)} %get-tuple-element.100.first_ref, s32[3]{0:T(128)} %get-tuple-element.99.last_ref, s32[768,1]{1,0:T(8,128)} %get-tuple-element.104.rows_ref, bf16[2048,2048]{1,0:T(8,128)(2,1)} %all-gather.5.cloned.1.call-done.table_ref, ...), custom_call_target="tpu_custom_call" | custom-call | flops 40000000000 | bytes 1024 | tf_op jit(solution)/shard_map/pallas_call | solution.py:154
  205.1 7.8 %shard_map.129 = (f32[768,896]{1,0:T(8,128)}, bf16[768,896]{1,0:T(8,128)(2,1)}) custom-call(bf16[768,2048]{1,0:T(8,128)(2,1)} %shard_map.128.a_ref.refs_0_.right_ref, bf16[2,896,2048]{2,1,0:T(8,128)(2,1)} %refs_4_.3, bf16[768,2048]{1,0:T(8,128)(2,1)} %shard_map.128.a_ref.refs_0_.right_ref), custom_call_target="tpu_custom_call" | custom-call | flops 40000000000 | bytes 1024 | tf_op jit(solution)/shard_map/pallas_call | solution.py:185
  213.4 8.6 %shard_map.130.refs_6_.refs_0_ = bf16[2,896,2048]{2,1,0:T(8,128)(2,1)} custom-call(bf16[768,896]{1,0:T(8,128)(2,1)} %get-tuple-element.56.refs_0_.left_ref, bf16[768,2048]{1,0:T(8,128)(2,1)} %shard_map.125.a_ref.refs_0_.right_ref, f32[768,896]{1,0:T(8,128)} %get-tuple-element.57.refs_0_.refs_4_), custom_call_target="tpu_custom_call" | custom-call | flops 40000000000 | bytes 1024 | tf_op jit(solution)/shard_map/pallas_call | solution.py:336
  222.1 13.6 %collective-permute-done.refs_1_.refs_3_ = bf16[2,768,896]{2,1,0:T(8,128)(2,1)} collective-permute-done((bf16[2,768,896]{2,1,0:T(8,128)(2,1)}, bf16[2,768,896]{2,1,0:T(8,128)(2,1)}, u32[]{:S(2)}, u32[]{:S(2)}) %collective-permute-start) | collective-permute-done | bytes 2752544 | tf_op jit(solution)/shard_map/ppermute | solution.py:466
  235.7 23.8 %shard_map.131 = (bf16[768,896]{1,0:T(8,128)(2,1)}, bf16[4,128,2048]{2,1,0:T(8,128)(2,1)}, bf16[4,128,2048]{2,1,0:T(8,128)(2,1)}, bf16[4,128,2048]{2,1,0:T(8,128)(2,1)}, bf16[4,128,2048]{2,1,0:T(8,128)(2,1)}) custom-call(s32[5,16]{1,0:T(8,128)} %select_bitcast_fusion.layout_ref, f32[768,1]{1,0:T(8,128)} %get-tuple-element.102.weight_ref, ...), custom_call_target="tpu_custom_call" | custom-call | flops 40000000000 | bytes 1024 | tf_op jit(solution)/shard_map/pallas_call | solution.py:309
  260.0 8.6 %shard_map.132.refs_2_ = bf16[2,896,2048]{2,1,0:T(8,128)(2,1)} custom-call(bf16[768,896]{1,0:T(8,128)(2,1)} %get-tuple-element.62.left_ref.refs_1_, bf16[768,2048]{1,0:T(8,128)(2,1)} %shard_map.128.a_ref.refs_0_.right_ref, bf16[2,896,2048]{2,1,0:T(8,128)(2,1)} %shard_map.130.refs_6_.refs_0_, ...), custom_call_target="tpu_custom_call", output_to_operand_aliasing={{}: (2, {})} | custom-call | flops 40000000000 | bytes 1024 | tf_op jit(solution)/shard_map/pallas_call | solution.py:336
  275.9 17.2 %shard_map.134 = (bf16[768,896]{1,0:T(8,128)(2,1)}, bf16[768,896]{1,0:T(8,128)(2,1)}, f32[880,2048]{1,0:T(8,128)}) custom-call(f32[768,1]{1,0:T(8,128)} %get-tuple-element.101.weight_ref, f32[768,896]{1,0:T(8,128)} %get-tuple-element.48.refs_0_, bf16[768,896]{1,0:T(8,128)(2,1)} %collective-permute-done.1.refs_1_, ...), custom_call_target="tpu_custom_call" | custom-call | flops 40000000000 | bytes 1024 | tf_op jit(solution)/shard_map/pallas_call | solution.py:309
  297.6 7.1 %shard_map.136.refs_3_.refs_0_ = bf16[2,2048,896]{2,1,0:T(8,128)(2,1)} custom-call(bf16[768,2048]{1,0:T(8,128)(2,1)} %shard_map.120.a_ref.refs_0_.left_ref, bf16[768,896]{1,0:T(8,128)(2,1)} %get-tuple-element.66.refs_3_.right_ref, bf16[1,128,2048]{2,1,0:T(8,128)(2,1)} %shard_map.135.refs_0_), custom_call_target="tpu_custom_call" | custom-call | flops 40000000000 | bytes 1024 | tf_op jit(solution)/shard_map/pallas_call | solution.py:336
  306.5 4.2 collective-permute-done.9.refs_2_
  311.7 3.4 shard_map.137
  316.0 7.1 %shard_map.138.refs_9_.refs_0_ = bf16[2,2048,896]{2,1,0:T(8,128)(2,1)} custom-call(bf16[768,2048]{1,0:T(8,128)(2,1)} %shard_map.120.a_ref.refs_0_.left_ref, bf16[768,896]{1,0:T(8,128)(2,1)} %get-tuple-element.72.right_ref, bf16[1,128,2048]{2,1,0:T(8,128)(2,1)} %get-tuple-element.68.refs_0_), custom_call_target="tpu_custom_call" | custom-call | flops 40000000000 | bytes 1024 | tf_op jit(solution)/shard_map/pallas_call | solution.py:336
  326.1 30.4 %shard_map.139 = (bf16[768,896]{1,0:T(8,128)(2,1)}, bf16[768,896]{1,0:T(8,128)(2,1)}, bf16[4,128,2048]{2,1,0:T(8,128)(2,1)}, bf16[4,128,2048]{2,1,0:T(8,128)(2,1...) custom-call(s32[5,16]{1,0:T(8,128)} %select_bitcast_fusion.layout_ref, ...), custom_call_target="tpu_custom_call" | custom-call | flops 40000000000 | bytes 1024 | tf_op jit(solution)/shard_map/pallas_call | solution.py:309
  358.2 4.7 %shard_map.140.refs_2_ = bf16[128,2048]{1,0:T(8,128)(2,1)} custom-call(f32[128,128]{1,0:T(8,128)} %compare_convert_fusion.1.hot_ref, bf16[4,128,2048]{2,1,0:T(8,128)(2,1)} %get-tuple-element.58.refs_0_, bf16[4,128,2048]{2,1,0:T(8,128)(2,1)} %copy-done.3, bf16[1,128,2048]{2,1,0:T(8,128)(2,1)} %collective-permute-done.5.refs_2_, ...), custom_call_target="tpu_custom_call" | custom-call | flops 40000000000 | bytes 1024 | tf_op jit(solution)/shard_map/pallas_call | solution.py:424
  368.3 7.1 %shard_map.142.refs_3_ = bf16[2,2048,896]{2,1,0:T(8,128)(2,1)} custom-call(bf16[768,2048]{1,0:T(8,128)(2,1)} %shard_map.123.a_ref.refs_0_.left_ref, bf16[768,896]{1,0:T(8,128)(2,1)} %get-tuple-element.73.refs_6_.right_ref, bf16[2,2048,896]{2,1,0:T(8,128)(2,1)} %shard_map.136.refs_3_.refs_0_, ...), custom_call_target="tpu_custom_call", output_to_operand_aliasing={{}: (2, {})} | custom-call | flops 40000000000 | bytes 1024 | tf_op jit(solution)/shard_map/pallas_call | solution.py:336
  377.4 5.3 %collective-permute-done.16.refs_2_ = bf16[1,128,2048]{2,1,0:T(8,128)(2,1)S(1)} collective-permute-done((bf16[1,128,2048]{2,1,0:T(8,128)(2,1)}, bf16[1,128,2048]{2,1,0:T(8,128)(2,1)S(1)}, u32[]{:S(2)}, u32[]{:S(2)}) %collective-permute-start.16) | collective-permute-done | bytes 524320 | tf_op jit(solution)/shard_map/ppermute | solution.py:367
  386.6 7.1 %shard_map.144.refs_3_ = bf16[2,2048,896]{2,1,0:T(8,128)(2,1)} custom-call(bf16[768,2048]{1,0:T(8,128)(2,1)} %shard_map.123.a_ref.refs_0_.left_ref, bf16[768,896]{1,0:T(8,128)(2,1)} %get-tuple-element.81.right_ref, bf16[2,2048,896]{2,1,0:T(8,128)(2,1)} %shard_map.138.refs_9_.refs_0_, ...), custom_call_target="tpu_custom_call", output_to_operand_aliasing={{}: (2, {})} | custom-call | flops 40000000000 | bytes 1024 | tf_op jit(solution)/shard_map/pallas_call | solution.py:336
  393.7 11.5 %collective-permute-done.18.refs_2_ = bf16[2,128,2048]{2,1,0:T(8,128)(2,1)S(1)} collective-permute-done((bf16[2,128,2048]{2,1,0:T(8,128)(2,1)S(1)}, bf16[2,128,2048]{2,1,0:T(8,128)(2,1)S(1)}, u32[]{:S(2)}, u32[]{:S(2)}) %collective-permute-start.18) | collective-permute-done | bytes 1048608 | tf_op jit(solution)/shard_map/ppermute | solution.py:367
  409.6 3.8 collective-permute-start.20
  415.6 10.9 %collective-permute-done.19.refs_4_ = bf16[1,128,2048]{2,1,0:T(8,128)(2,1)S(1)} collective-permute-done((bf16[1,128,2048]{2,1,0:T(8,128)(2,1)}, bf16[1,128,2048]{2,1,0:T(8,128)(2,1)S(1)}, u32[]{:S(2)}, u32[]{:S(2)}) %collective-permute-start.19) | collective-permute-done | bytes 524320 | tf_op jit(solution)/shard_map/ppermute | solution.py:367
  426.5 6.8 %collective-permute-done.20.refs_5_ = bf16[1,128,2048]{2,1,0:T(8,128)(2,1)S(1)} collective-permute-done((bf16[1,128,2048]{2,1,0:T(8,128)(2,1)}, bf16[1,128,2048]{2,1,0:T(8,128)(2,1)S(1)}, u32[]{:S(2)}, u32[]{:S(2)}) %collective-permute-start.20) | collective-permute-done | bytes 524320 | tf_op jit(solution)/shard_map/ppermute | solution.py:367
  434.1 4.7 %shard_map.146 = bf16[128,2048]{1,0:T(8,128)(2,1)} custom-call(f32[128,128]{1,0:T(8,128)} %compare_convert_fusion.1.hot_ref, bf16[4,128,2048]{2,1,0:T(8,128)(2,1)} %get-tuple-element.74.refs_0_, bf16[4,128,2048]{2,1,0:T(8,128)(2,1)} %copy-done.4, bf16[1,128,2048]{2,1,0:T(8,128)(2,1)} %copy-done.13, bf16[1,128,2048]{2,1,0:T(8,128)(2,1)} %copy-done.17, ...), custom_call_target="tpu_custom_call" | custom-call | flops 40000000000 | bytes 1024 | tf_op jit(solution)/shard_map/pallas_call | solution.py:424
  (127 shorter events, 66.3 us)
Async XLA Ops:
  7.2 80.6 %all-gather.3.cloned.1.call-start = ((), (), s32[]{:S(2)}) async-start(), calls=%async_computation | async-start | bytes 8912896 | tf_op jit(solution)/shard_map/all_gather | solution.py:476
  7.9 155.2 %all-gather.5.cloned.1.call-start = ((), (), s32[]{:S(2)}) async-start(), calls=%async_computation.1 | async-start | bytes 8912896 | tf_op jit(solution)/shard_map/all_gather | solution.py:477
  12.6 11.3 %copy-start.1 = (s32[2,768]{1,0:T(2,128)S(1)}, s32[2,768]{1,0:T(2,128)}, u32[]{:S(2)}) copy-start(s32[2,768]{1,0:T(2,128)} %param.11) | copy-start | bytes 18436
  19.0 5.5 %copy-start.2 = (f32[2,1,768]{2,1,0:T(1,128)S(1)}, f32[2,1,768]{2,1,0:T(1,128)}, u32[]{:S(2)}) copy-start(f32[2,1,768]{2,1,0:T(1,128)} %get-tuple-element.45) | copy-start | bytes 18436
  113.8 69.2 %collective-permute-start.2 = (bf16[768,896]{1,0:T(8,128)(2,1)}, bf16[768,896]{1,0:T(8,128)(2,1)}, u32[]{:S(2)}, u32[]{:S(2)}) collective-permute-start(bf16[768,896]{1,0:T(8,128)(2,1)} %get-tuple-element.53), channel_id=1, source_target_pairs={{0,1},{1,0},{2,3},{3,2},{4,5},{5,4},{6,7},{7,6},{8,9},{9,8},{10,11... | collective-permute-start | bytes 4128776 | tf_op jit(solution)/shard_map/ppermute | solution.py:466
  115.3 67.7 %collective-permute-start.1 = (bf16[768,896]{1,0:T(8,128)(2,1)}, bf16[768,896]{1,0:T(8,128)(2,1)}, u32[]{:S(2)}, u32[]{:S(2)}) collective-permute-start(bf16[768,896]{1,0:T(8,128)(2,1)} %get-tuple-element.52), channel_id=1, source_target_pairs={{0,1},{1,0},{2,3},{3,2},{4,5},{5,4},{6,7},{7,6},{8,9},{9,8},{10,11... | collective-permute-start | bytes 4128776 | tf_op jit(solution)/shard_map/ppermute | solution.py:466
  139.9 95.8 %collective-permute-start = (bf16[2,768,896]{2,1,0:T(8,128)(2,1)}, bf16[2,768,896]{2,1,0:T(8,128)(2,1)}, u32[]{:S(2)}, u32[]{:S(2)}) collective-permute-start(bf16[2,768,896]{2,1,0:T(8,128)(2,1)} %get-tuple-element.51), channel_id=1, source_target_pairs={{0,1},{1,0},{2,3},{3,2},{4,5},{5,4},{6,7},{7,6},{8,9},{9,8},{10,11... | collective-permute-start | bytes 8257544 | tf_op jit(solution)/shard_map/ppermute | solution.py:466
  181.6 93.7 %collective-permute-start.7 = (bf16[768,896]{1,0:T(8,128)(2,1)}, bf16[768,896]{1,0:T(8,128)(2,1)}, u32[]{:S(2)}, u32[]{:S(2)}) collective-permute-start(bf16[768,896]{1,0:T(8,128)(2,1)} %get-tuple-element.65), channel_id=1, source_target_pairs={{0,1},{1,0},{2,3},{3,2},{4,5},{5,4},{6,7},{7,6},{8,9},{9,8},{10,11... | collective-permute-start | bytes 4128776 | tf_op jit(solution)/shard_map/ppermute | solution.py:466
  212.9 113.2 %collective-permute-start.12 = (bf16[768,896]{1,0:T(8,128)(2,1)}, bf16[768,896]{1,0:T(8,128)(2,1)}, u32[]{:S(2)}, u32[]{:S(2)}) collective-permute-start(bf16[768,896]{1,0:T(8,128)(2,1)} %get-tuple-element.70), channel_id=1, source_target_pairs={{0,1},{1,0},{2,3},{3,2},{4,5},{5,4},{6,7},{7,6},{8,9},{9,8},{10,11... | collective-permute-start | bytes 4128776 | tf_op jit(solution)/shard_map/ppermute | solution.py:466
  259.4 9.2 %collective-permute-start.4 = (bf16[4,128,2048]{2,1,0:T(8,128)(2,1)}, bf16[4,128,2048]{2,1,0:T(8,128)(2,1)S(1)}, u32[]{:S(2)}, u32[]{:S(2)}) collective-permute-start(bf16[4,128,2048]{2,1,0:T(8,128)(2,1)} %get-tuple-element.61), channel_id=1, source_target_pairs={{0,2},{2,0},{4,6},{6,4},{8,10},{10,8},{12,14},{14,12},{16,18},{18,... | collective-permute-start | bytes 6291464 | tf_op jit(solution)/shard_map/ppermute | solution.py:367
  259.5 33.5 %collective-permute-start.3 = (bf16[4,128,2048]{2,1,0:T(8,128)(2,1)}, bf16[4,128,2048]{2,1,0:T(8,128)(2,1)S(1)}, u32[]{:S(2)}, u32[]{:S(2)}) collective-permute-start(bf16[4,128,2048]{2,1,0:T(8,128)(2,1)} %get-tuple-element.59), channel_id=1, source_target_pairs={{0,2},{2,0},{4,6},{6,4},{8,10},{10,8},{12,14},{14,12},{16,18},{18,... | collective-permute-start | bytes 6291464 | tf_op jit(solution)/shard_map/ppermute | solution.py:367
  273.3 19.8 %collective-permute-start.6 = (bf16[1,128,2048]{2,1,0:T(8,128)(2,1)}, bf16[1,128,2048]{2,1,0:T(8,128)(2,1)S(1)}, u32[]{:S(2)}, u32[]{:S(2)}) collective-permute-start(bf16[1,128,2048]{2,1,0:T(8,128)(2,1)} %get-tuple-element.64.refs_8_), channel_id=1, source_target_pairs={{0,4},{2,6},{4,0},{6,2},{8,12},{10,14},{12,8},{14,10},{16,20},{18,... | collective-permute-start | bytes 1572872 | tf_op jit(solution)/shard_map/ppermute | solution.py:367
  273.8 36.9 %collective-permute-start.9 = (bf16[2,128,2048]{2,1,0:T(8,128)(2,1)}, bf16[2,128,2048]{2,1,0:T(8,128)(2,1)S(1)}, u32[]{:S(2)}, u32[]{:S(2)}) collective-permute-start(bf16[2,128,2048]{2,1,0:T(8,128)(2,1)} %get-tuple-element.67), channel_id=1, source_target_pairs={{0,4},{2,6},{4,0},{6,2},{8,12},{10,14},{12,8},{14,10},{16,20},{18,... | collective-permute-start | bytes 3145736 | tf_op jit(solution)/shard_map/ppermute | solution.py:367
  275.3 81.3 %collective-permute-start.5 = (bf16[1,128,2048]{2,1,0:T(8,128)(2,1)}, bf16[1,128,2048]{2,1,0:T(8,128)(2,1)}, u32[]{:S(2)}, u32[]{:S(2)}) collective-permute-start(bf16[1,128,2048]{2,1,0:T(8,128)(2,1)} %get-tuple-element.63), channel_id=1, source_target_pairs={{0,4},{2,6},{4,0},{6,2},{8,12},{10,14},{12,8},{14,10},{16,20},{18,... | collective-permute-start | bytes 1572872 | tf_op jit(solution)/shard_map/ppermute | solution.py:367
  297.6 7.1 %copy-start.11 = (bf16[1,128,2048]{2,1,0:T(8,128)(2,1)S(1)}, bf16[1,128,2048]{2,1,0:T(8,128)(2,1)}, u32[]{:S(2)}) copy-start(bf16[1,128,2048]{2,1,0:T(8,128)(2,1)} %shard_map.135.refs_0_) | copy-start | bytes 1572868
  304.8 52.3 %collective-permute-start.8 = (bf16[1,128,2048]{2,1,0:T(8,128)(2,1)S(1)}, bf16[1,128,2048]{2,1,0:T(8,128)(2,1)S(1)}, u32[]{:S(2)}, u32[]{:S(2)}) collective-permute-start(bf16[1,128,2048]{2,1,0:T(8,128)(2,1)S(1)} %copy-done.11), channel_id=1, source_target_pairs={{0,16},{2,18},{4,20},{6,22},{8,24},{10,26},{12,28},{14,30},{16,0},... | collective-permute-start | bytes 1572872 | tf_op jit(solution)/shard_map/ppermute | solution.py:367
  315.1 42.0 %collective-permute-start.10 = (bf16[1,128,2048]{2,1,0:T(8,128)(2,1)}, bf16[1,128,2048]{2,1,0:T(8,128)(2,1)S(1)}, u32[]{:S(2)}, u32[]{:S(2)}) collective-permute-start(bf16[1,128,2048]{2,1,0:T(8,128)(2,1)} %get-tuple-element.68.refs_0_), channel_id=1, source_target_pairs={{0,8},{2,10},{4,12},{6,14},{8,16},{10,18},{12,20},{14,22},{16,24},... | collective-permute-start | bytes 1572872 | tf_op jit(solution)/shard_map/ppermute | solution.py:367
  316.0 7.1 %copy-start.15 = (bf16[1,128,2048]{2,1,0:T(8,128)(2,1)S(1)}, bf16[1,128,2048]{2,1,0:T(8,128)(2,1)}, u32[]{:S(2)}) copy-start(bf16[1,128,2048]{2,1,0:T(8,128)(2,1)} %get-tuple-element.69) | copy-start | bytes 1572868
  323.1 34.0 %collective-permute-start.11 = (bf16[1,128,2048]{2,1,0:T(8,128)(2,1)S(1)}, bf16[1,128,2048]{2,1,0:T(8,128)(2,1)S(1)}, u32[]{:S(2)}, u32[]{:S(2)}) collective-permute-start(bf16[1,128,2048]{2,1,0:T(8,128)(2,1)S(1)} %copy-done.15), channel_id=1, source_target_pairs={{0,24},{2,26},{4,28},{6,30},{8,0},{10,2},{12,4},{14,6},{16,8},{18,... | collective-permute-start | bytes 1572872 | tf_op jit(solution)/shard_map/ppermute | solution.py:367
  356.5 6.4 %collective-permute-start.14 = (bf16[4,128,2048]{2,1,0:T(8,128)(2,1)}, bf16[4,128,2048]{2,1,0:T(8,128)(2,1)S(1)}, u32[]{:S(2)}, u32[]{:S(2)}) collective-permute-start(bf16[4,128,2048]{2,1,0:T(8,128)(2,1)} %get-tuple-element.77), channel_id=1, source_target_pairs={{0,2},{2,0},{4,6},{6,4},{8,10},{10,8},{12,14},{14,12},{16,18},{18,... | collective-permute-start | bytes 6291464 | tf_op jit(solution)/shard_map/ppermute | solution.py:367
  356.6 20.9 %collective-permute-start.13 = (bf16[4,128,2048]{2,1,0:T(8,128)(2,1)}, bf16[4,128,2048]{2,1,0:T(8,128)(2,1)S(1)}, u32[]{:S(2)}, u32[]{:S(2)}) collective-permute-start(bf16[4,128,2048]{2,1,0:T(8,128)(2,1)} %get-tuple-element.75), channel_id=1, source_target_pairs={{0,2},{2,0},{4,6},{6,4},{8,10},{10,8},{12,14},{14,12},{16,18},{18,... | collective-permute-start | bytes 6291464 | tf_op jit(solution)/shard_map/ppermute | solution.py:367
  367.7 7.7 %copy-start.8 = (bf16[2,128,2048]{2,1,0:T(8,128)(2,1)S(1)}, bf16[2,128,2048]{2,1,0:T(8,128)(2,1)}, u32[]{:S(2)}) copy-start(bf16[2,128,2048]{2,1,0:T(8,128)(2,1)} %get-tuple-element.80) | copy-start | bytes 3145732
  367.7 9.2 %copy-start.14 = (bf16[1,128,2048]{2,1,0:T(8,128)(2,1)S(1)}, bf16[1,128,2048]{2,1,0:T(8,128)(2,1)}, u32[]{:S(2)}) copy-start(bf16[1,128,2048]{2,1,0:T(8,128)(2,1)} %get-tuple-element.78) | copy-start | bytes 1572868
  367.7 15.1 %collective-permute-start.16 = (bf16[1,128,2048]{2,1,0:T(8,128)(2,1)}, bf16[1,128,2048]{2,1,0:T(8,128)(2,1)S(1)}, u32[]{:S(2)}, u32[]{:S(2)}) collective-permute-start(bf16[1,128,2048]{2,1,0:T(8,128)(2,1)} %get-tuple-element.79.refs_1_), channel_id=1, source_target_pairs={{0,4},{2,6},{4,0},{6,2},{8,12},{10,14},{12,8},{14,10},{16,20},{18,... | collective-permute-start | bytes 1572872 | tf_op jit(solution)/shard_map/ppermute | solution.py:367
  375.4 29.8 %collective-permute-start.18 = (bf16[2,128,2048]{2,1,0:T(8,128)(2,1)S(1)}, bf16[2,128,2048]{2,1,0:T(8,128)(2,1)S(1)}, u32[]{:S(2)}, u32[]{:S(2)}) collective-permute-start(bf16[2,128,2048]{2,1,0:T(8,128)(2,1)S(1)} %copy-done.8), channel_id=1, source_target_pairs={{0,4},{2,6},{4,0},{6,2},{8,12},{10,14},{12,8},{14,10},{16,20},{18,... | collective-permute-start | bytes 3145736 | tf_op jit(solution)/shard_map/ppermute | solution.py:367
  376.9 38.7 %collective-permute-start.15 = (bf16[1,128,2048]{2,1,0:T(8,128)(2,1)S(1)}, bf16[1,128,2048]{2,1,0:T(8,128)(2,1)S(1)}, u32[]{:S(2)}, u32[]{:S(2)}) collective-permute-start(bf16[1,128,2048]{2,1,0:T(8,128)(2,1)S(1)} %copy-done.14), channel_id=1, source_target_pairs={{0,4},{2,6},{4,0},{6,2},{8,12},{10,14},{12,8},{14,10},{16,20},{18,... | collective-permute-start | bytes 1572872 | tf_op jit(solution)/shard_map/ppermute | solution.py:367
  386.6 29.0 %collective-permute-start.17 = (bf16[1,128,2048]{2,1,0:T(8,128)(2,1)}, bf16[1,128,2048]{2,1,0:T(8,128)(2,1)S(1)}, u32[]{:S(2)}, u32[]{:S(2)}) collective-permute-start(bf16[1,128,2048]{2,1,0:T(8,128)(2,1)} %shard_map.143.refs_1_), channel_id=1, source_target_pairs={{0,16},{2,18},{4,20},{6,22},{8,24},{10,26},{12,28},{14,30},{16,0},... | collective-permute-start | bytes 1572872 | tf_op jit(solution)/shard_map/ppermute | solution.py:367
  409.6 16.9 %collective-permute-start.19 = (bf16[1,128,2048]{2,1,0:T(8,128)(2,1)}, bf16[1,128,2048]{2,1,0:T(8,128)(2,1)S(1)}, u32[]{:S(2)}, u32[]{:S(2)}) collective-permute-start(bf16[1,128,2048]{2,1,0:T(8,128)(2,1)} %get-tuple-element.82.refs_6_), channel_id=1, source_target_pairs={{0,8},{2,10},{4,12},{6,14},{8,16},{10,18},{12,20},{14,22},{16,24},... | collective-permute-start | bytes 1572872 | tf_op jit(solution)/shard_map/ppermute | solution.py:367
  409.6 23.6 %collective-permute-start.20 = (bf16[1,128,2048]{2,1,0:T(8,128)(2,1)}, bf16[1,128,2048]{2,1,0:T(8,128)(2,1)S(1)}, u32[]{:S(2)}, u32[]{:S(2)}) collective-permute-start(bf16[1,128,2048]{2,1,0:T(8,128)(2,1)} %get-tuple-element.83), channel_id=1, source_target_pairs={{0,24},{2,26},{4,28},{6,30},{8,0},{10,2},{12,4},{14,6},{16,8},{18,... | collective-permute-start | bytes 1572872 | tf_op jit(solution)/shard_map/ppermute | solution.py:367
  415.6 17.7 %copy-start.13 = (bf16[1,128,2048]{2,1,0:T(8,128)(2,1)}, bf16[1,128,2048]{2,1,0:T(8,128)(2,1)S(1)}, u32[]{:S(2)}) copy-start(bf16[1,128,2048]{2,1,0:T(8,128)(2,1)S(1)} %collective-permute-done.15.refs_2_) | copy-start | bytes 1572868
  415.6 17.7 %copy-start.17 = (bf16[1,128,2048]{2,1,0:T(8,128)(2,1)}, bf16[1,128,2048]{2,1,0:T(8,128)(2,1)S(1)}, u32[]{:S(2)}) copy-start(bf16[1,128,2048]{2,1,0:T(8,128)(2,1)S(1)} %collective-permute-done.17.refs_3_) | copy-start | bytes 1572868
  426.5 6.8 %copy-start.19 = (bf16[1,128,2048]{2,1,0:T(8,128)(2,1)}, bf16[1,128,2048]{2,1,0:T(8,128)(2,1)S(1)}, u32[]{:S(2)}) copy-start(bf16[1,128,2048]{2,1,0:T(8,128)(2,1)S(1)} %collective-permute-done.19.refs_4_) | copy-start | bytes 1572868
  (13 other events, 21.2 us)
Sparse Core Ops, SparseCore 0:
  10.2 77.5 all-gather.2
  89.9 73.1 all-gather.4
